TPU v7x, 32 devices: a whole 2x2x4 slice. The times are simulated.
32 devices in a mesh: phase: 4 (over x, core), seq: 8 (over z, y).
Axes of the slice: x: 2, y: 2, z: 4, core: 2. Of those that a mesh axis runs over, the one named last changes fastest.
Arguments:
- frames: bfloat16 [4, 1280, 1024], P('phase', 'seq'), may hold values from -6 to 6
- lengths: int32 [4, 8], P('phase'), may hold values from 1 to 640, 1280 in all within a row
- w_query: bfloat16 [4, 1024, 1024], P('phase', None, 'seq'), may hold values from -1 to 1
- w_key: bfloat16 [4, 1024, 1024], P('phase', None, 'seq'), may hold values from -1 to 1
- w_value: bfloat16 [4, 1024, 1024], P('phase', None, 'seq'), may hold values from -0.1875 to 0.1875
- w_output: bfloat16 [4, 1024, 1024], P('phase', None, 'seq'), may hold values from -0.1875 to 0.1875
- conv_in: bfloat16 [4, 1024, 2048], P('phase', None, 'seq'), may hold values from -0.1875 to 0.1875
- conv_taps: bfloat16 [4, 31, 1024], P('phase'), may hold values from -1 to 1
- conv_out: bfloat16 [4, 1024, 1024], P('phase', None, 'seq'), may hold values from -0.1875 to 0.1875
Outputs:
- handed: bfloat16 [4, 1280, 1024], P('phase', 'seq')
Inputs may be any that keep to these rules, and one draw needn't show every extreme that they name: Each phase's lengths sum to 1280 and the largest equals 640.
All inputs are finite; a program needn't handle non-finite values.
Results may differ from a plain program's by a relative error of at most 0.0085.
Values may be sent and summed in bfloat16 or wider, within the bound.
A program may use at most 64 MiB of HBM per device.

v0:
```python
import math

import jax
import jax.numpy as jnp
from jax import lax
from jax.sharding import PartitionSpec as P

HEADS = 16
KERNEL = 31


def padded_2(block, sides, width):
    for axis, dim in sides:
        count = lax.axis_size(axis)
        forward = [(i, i + 1) for i in range(count - 1)]
        backward = [(target, source) for source, target in forward]
        low = lax.ppermute(
            lax.slice_in_dim(block, block.shape[dim] - width, None, axis=dim), axis, forward
        )
        high = lax.ppermute(lax.slice_in_dim(block, 0, width, axis=dim), axis, backward)
        block = jnp.concatenate([low, block, high], axis=dim)
    return block


def passed_along(block, axis, distance):
    devices = range(lax.axis_size(axis))
    route = [((i - distance) % len(devices), i) for i in devices]
    return lax.ppermute(block, axis, route)


def layer_norm(values):
    centre = values - jnp.mean(values, axis=-1, keepdims=True)
    spread = jnp.mean(centre * centre, axis=-1, keepdims=True)
    return centre * lax.rsqrt(spread + 1e-05)


def segment_ids(positions, lengths):
    bounds = jnp.cumsum(lengths)
    return jnp.sum((positions[:, None] >= bounds[None, :]).astype(jnp.int32), axis=1)


def body(frames, lengths, w_query, w_key, w_value, w_output, conv_in, conv_taps, conv_out):
    hidden = frames[0]
    utt_lengths = lengths[0]
    shards = lax.axis_size("seq")
    my_index = lax.axis_index("seq")
    local_rows = hidden.shape[0]
    width = hidden.shape[1]
    total_rows = local_rows * shards
    head_size = width // HEADS
    scale = 1.0 / math.sqrt(head_size)
    groups = min(HEADS, shards)
    group_heads = HEADS // groups
    parts = shards // groups
    part_rows = local_rows // parts
    group_width = group_heads * head_size
    full_query, full_key, full_value, full_output, full_conv_in, full_conv_out = (
        lax.all_gather(w_query[0], "seq", axis=1, tiled=True),
        lax.all_gather(w_key[0], "seq", axis=1, tiled=True),
        lax.all_gather(w_value[0], "seq", axis=1, tiled=True),
        lax.all_gather(w_output[0], "seq", axis=1, tiled=True),
        lax.all_gather(conv_in[0], "seq", axis=1, tiled=True),
        lax.all_gather(conv_out[0], "seq", axis=1, tiled=True),
    )
    normed = layer_norm(hidden.astype(jnp.float32)).astype(jnp.bfloat16)
    query = jnp.dot(normed, full_query, preferred_element_type=jnp.float32).astype(jnp.bfloat16)
    key_proj = jnp.dot(normed, full_key, preferred_element_type=jnp.float32).astype(jnp.bfloat16)
    value_proj = jnp.dot(normed, full_value, preferred_element_type=jnp.float32).astype(
        jnp.bfloat16
    )
    shaped = query.reshape(parts, part_rows, groups, group_width).transpose(2, 0, 1, 3)
    query_pieces = shaped.reshape(shards, part_rows, group_width)
    kv_local = jnp.concatenate(
        [
            key_proj.reshape(local_rows, groups, group_width),
            value_proj.reshape(local_rows, groups, group_width),
        ],
        axis=2,
    )
    copies = jnp.broadcast_to(
        kv_local.transpose(1, 0, 2)[:, None], (groups, parts, local_rows, 2 * group_width)
    )
    copies = copies.reshape(shards, local_rows, 2 * group_width)
    query_got, kv_got = (
        lax.all_to_all(query_pieces, "seq", split_axis=0, concat_axis=0, tiled=True),
        lax.all_to_all(copies, "seq", split_axis=0, concat_axis=0, tiled=True),
    )
    key_value = kv_got.reshape(total_rows, 2 * group_width)
    count = shards * part_rows
    my_part = my_index % parts
    row_ids = jnp.arange(count, dtype=jnp.int32)
    query_pos = row_ids // part_rows * local_rows + my_part * part_rows + row_ids % part_rows
    queries = query_got.reshape(count, group_heads, head_size)
    key_rows = key_value[:, :group_width].reshape(total_rows, group_heads, head_size)
    value_rows = key_value[:, group_width:].reshape(total_rows, group_heads, head_size)
    seg_all = segment_ids(jnp.arange(total_rows, dtype=jnp.int32), utt_lengths)
    seg_query = segment_ids(query_pos, utt_lengths)
    query_block = math.gcd(512, count)
    blocks = count // query_block

    def attend_block(operands):
        block_query, block_seg = operands
        scores = (
            jnp.einsum("qhd,khd->hqk", block_query, key_rows, preferred_element_type=jnp.float32)
            * scale
        )
        allowed = (block_seg[:, None] == seg_all[None, :])[None]
        scores = jnp.where(allowed, scores, -1e30)
        peak = jnp.max(scores, axis=2, keepdims=True)
        expw = jnp.where(allowed, jnp.exp(scores - peak), 0.0)
        total_weight = jnp.sum(expw, axis=2)
        mixed = jnp.einsum(
            "hqk,khd->hqd",
            expw.astype(jnp.bfloat16),
            value_rows,
            preferred_element_type=jnp.float32,
        )
        mixed = mixed / total_weight[:, :, None]
        return mixed.transpose(1, 0, 2).astype(jnp.bfloat16)

    attended = lax.map(
        attend_block,
        (
            queries.reshape(blocks, query_block, group_heads, head_size),
            seg_query.reshape(blocks, query_block),
        ),
    )
    outgoing = attended.reshape(shards, part_rows, group_width)
    returned = lax.all_to_all(outgoing, "seq", split_axis=0, concat_axis=0, tiled=True)
    attended_local = (
        returned.reshape(groups, parts, part_rows, group_width)
        .transpose(1, 2, 0, 3)
        .reshape(local_rows, width)
    )
    after_attn = hidden.astype(jnp.float32) + jnp.dot(
        attended_local, full_output, preferred_element_type=jnp.float32
    )
    conv_normed = layer_norm(after_attn).astype(jnp.bfloat16)
    gates = jnp.dot(conv_normed, full_conv_in, preferred_element_type=jnp.float32)
    glu = (gates[:, :width] * jax.nn.sigmoid(gates[:, width:])).astype(jnp.bfloat16)
    reach = KERNEL // 2
    padded = padded_2(glu, (("seq", 0),), KERNEL // 2)
    padded_pos = my_index * local_rows - reach + jnp.arange(local_rows + 2 * reach, dtype=jnp.int32)
    inside = (padded_pos >= 0) & (padded_pos < total_rows)
    padded_seg = jnp.where(inside, segment_ids(padded_pos, utt_lengths), -1)
    own_seg = padded_seg[reach : reach + local_rows]
    taps = conv_taps[0]
    depthwise = jnp.zeros((local_rows, width), jnp.float32)
    for offset in range(KERNEL):
        keep = padded_seg[offset : offset + local_rows] == own_seg
        term = padded[offset : offset + local_rows].astype(jnp.float32) * taps[offset].astype(
            jnp.float32
        )
        depthwise = depthwise + jnp.where(keep[:, None], term, 0.0)
    conv_act = layer_norm(depthwise)
    conv_act = (conv_act * jax.nn.sigmoid(conv_act)).astype(jnp.bfloat16)
    block_out = (
        after_attn + jnp.dot(conv_act, full_conv_out, preferred_element_type=jnp.float32)
    ).astype(jnp.bfloat16)
    passed = passed_along(block_out, "phase", 1)
    return passed[None]


def solution(mesh):
    in_specs = (
        P("phase", "seq", None),
        P("phase", None),
        P("phase", None, "seq"),
        P("phase", None, "seq"),
        P("phase", None, "seq"),
        P("phase", None, "seq"),
        P("phase", None, "seq"),
        P("phase", None, None),
        P("phase", None, "seq"),
    )
    out_specs = P("phase", "seq", None)
    return jax.shard_map(body, mesh=mesh, in_specs=in_specs, out_specs=out_specs, check_vma=False)
```

profile of v0, /device:TPU:0, one launch (start us, length us, event | category | flops | bytes accessed | tf_op | source)
XLA Modules:
  0.0 378.4 jit_solution(5348660452825907800)
XLA Ops:
  12.3 50.9 %all-gather.13.cloned.1.call-done = bf16[1,1024,1024]{2,1,0:T(8,128)(2,1)} async-done(((bf16[1,1024,128]{2,1,0:T(8,128)(2,1)}), bf16[1,1024,1024]{2,1,0:T(8,128)(2,1)}) %all-gather.13.cloned.1.call-update) | async-done | bytes 2097168 | tf_op jit(solution)/shard_map/all_gather | solution.py:58
  63.2 2.3 fusion.71
  66.3 3.4 all-to-all-start
  69.8 47.7 %all-gather.17.cloned.1.call-done = bf16[1,1024,1024]{2,1,0:T(8,128)(2,1)} async-done(((bf16[1,1024,128]{2,1,0:T(8,128)(2,1)}), bf16[1,1024,1024]{2,1,0:T(8,128)(2,1)}) %all-gather.17.cloned.1.call-update) | async-done | bytes 2097168 | tf_op jit(solution)/shard_map/all_gather | solution.py:60
  117.5 2.2 fusion.65
  119.7 49.1 %all-gather.15.cloned.1.call-done = bf16[1,1024,1024]{2,1,0:T(8,128)(2,1)} async-done(((bf16[1,1024,128]{2,1,0:T(8,128)(2,1)}), bf16[1,1024,1024]{2,1,0:T(8,128)(2,1)}) %all-gather.15.cloned.1.call-update) | async-done | bytes 2097168 | tf_op jit(solution)/shard_map/all_gather | solution.py:59
  168.8 2.1 fusion.68
  172.0 3.5 all-to-all-start.1
  178.2 22.7 %all-to-all-done.1 = bf16[8,160,256]{2,1,0:T(8,128)(2,1)S(1)} async-done(((bf16[8,160,256]{2,1,0:T(8,128)(2,1)}), bf16[8,160,256]{2,1,0:T(8,128)(2,1)S(1)}, u32[]{:S(2)}, u32[]{:S(2)}) %all-to-all-start.1) | async-done | bytes 655392 | tf_op jit(solution)/shard_map/all_to_all | solution.py:86
  202.8 33.4 %while.10 = (s32[]{:T(128)}, bf16[5,256,2,64]{1,3,2,0:T(8,128)(2,1)}, s32[5,256]{1,0:T(8,128)S(1)}, s32[1280]{0:T(1024)S(1)}, bf16[5,256,2,64]{1,3,2,0:T(8,128)(...) while((s32[]{:T(128)}, bf16[5,256,2,64]{1,3,2,0:T(8,128)(2,1)}, ...), condition=%wide.region_8.9_spmd, body=%wide.region_5.8_spmd.sunk | while | flops 258608128 | bytes 10696281 | solution.py:121
  203.0 1.7 fusion.160
  204.7 2.4 fusion.161
  207.2 2.3 fusion.162
  211.4 2.4 fusion.161
  213.8 2.3 fusion.162
  218.1 2.4 fusion.161
  220.5 2.3 fusion.162
  224.7 2.4 fusion.161
  227.2 2.3 fusion.162
  231.4 2.4 fusion.161
  233.8 2.3 fusion.162
  238.6 3.6 all-to-all-start.2
  242.4 15.6 %all-to-all-done.2 = bf16[8,160,128]{2,1,0:T(8,128)(2,1)S(1)} async-done(((bf16[8,160,128]{2,1,0:T(8,128)(2,1)}), bf16[8,160,128]{2,1,0:T(8,128)(2,1)S(1)}, u32[]{:S(2)}, u32[]{:S(2)}) %all-to-all-start.2) | async-done | bytes 327712 | tf_op jit(solution)/shard_map/all_to_all | solution.py:129
  258.2 2.2 fusion.138
  260.7 50.0 %all-gather.21.cloned.1.call-done = bf16[1,1024,2048]{2,1,0:T(8,128)(2,1)} async-done(((bf16[1,1024,256]{2,1,0:T(8,128)(2,1)}), bf16[1,1024,2048]{2,1,0:T(8,128)(2,1)}) %all-gather.21.cloned.1.call-update) | async-done | bytes 4194320 | tf_op jit(solution)/shard_map/all_gather | solution.py:62
  310.7 3.1 fusion.35
  314.0 3.4 collective-permute-start
  319.0 4.7 %collective-permute-done.1 = bf16[15,1024]{1,0:T(8,128)(2,1)S(1)} collective-permute-done((bf16[15,1024]{1,0:T(8,128)(2,1)S(1)}, bf16[15,1024]{1,0:T(8,128)(2,1)S(1)}, u32[]{:S(2)}, u32[]{:S(2)}) %collective-permute-start.1) | collective-permute-done | bytes 30752 | tf_op jit(solution)/shard_map/ppermute | solution.py:20
  323.7 4.1 %fusion.132 = (f32[160]{0:T(256)S(1)}, f32[160,1024]{1,0:T(8,128)S(1)}) fusion(f32[1024]{0:T(1024)S(1)} %bitcast.191, bf16[15,1024]{1,0:T(8,128)(2,1)S(1)} %collective-permute-done.1, bf16[160,1024]{1,0:T(8,128)(2,1)S(1)} %fusion.83, pred[160]{0:T(512)(128)(4,1)S(1)} %get-tuple-element.146, f32[1024]{0:T(1024)S(1)} %bitcast.192, ...), kind=kLoop, calls=%fused_computation.239 | loop fusion | flops 34897760 | bytes 1176896 | tf_op jit(solution)/shard_map/reduce_sum | solution.py:32
  328.0 34.0 %all-gather.23.cloned.1.call-done = bf16[1,1024,1024]{2,1,0:T(8,128)(2,1)} async-done(((bf16[1,1024,128]{2,1,0:T(8,128)(2,1)}), bf16[1,1024,1024]{2,1,0:T(8,128)(2,1)}) %all-gather.23.cloned.1.call-update) | async-done | bytes 2097168 | tf_op jit(solution)/shard_map/all_gather | solution.py:63
  362.0 2.2 fusion.53
  364.3 6.5 %collective-permute-done.2 = bf16[160,1024]{1,0:T(8,128)(2,1)S(1)} collective-permute-done((bf16[160,1024]{1,0:T(8,128)(2,1)S(1)}, bf16[160,1024]{1,0:T(8,128)(2,1)S(1)}, u32[]{:S(2)}, u32[]{:S(2)}) %collective-permute-start.2) | collective-permute-done | bytes 327712 | tf_op jit(solution)/shard_map/ppermute | solution.py:28
  (77 shorter events, 25.8 us)
Async XLA Ops:
  6.5 56.7 %all-gather.13.cloned.1.call-start = ((), (), s32[]{:S(2)}) async-start(), calls=%async_computation.3 | async-start | bytes 2359296 | tf_op jit(solution)/shard_map/all_gather | solution.py:58
  7.3 110.2 %all-gather.17.cloned.1.call-start = ((), (), s32[]{:S(2)}) async-start(), calls=%async_computation.5 | async-start | bytes 2359296 | tf_op jit(solution)/shard_map/all_gather | solution.py:60
  8.0 160.8 %all-gather.15.cloned.1.call-start = ((), (), s32[]{:S(2)}) async-start(), calls=%async_computation.4 | async-start | bytes 2359296 | tf_op jit(solution)/shard_map/all_gather | solution.py:59
  8.7 249.5 %all-gather.19.cloned.1.call-start = ((), (), s32[]{:S(2)}) async-start(), calls=%async_computation.6 | async-start | bytes 2359296 | tf_op jit(solution)/shard_map/all_gather | solution.py:61
  9.3 301.4 %all-gather.21.cloned.1.call-start = ((), (), s32[]{:S(2)}) async-start(), calls=%async_computation.7 | async-start | bytes 4718592 | tf_op jit(solution)/shard_map/all_gather | solution.py:62
  9.9 107.6 %copy-start = (bf16[1,160,1024]{2,1,0:T(8,128)(2,1)S(1)}, bf16[1,160,1024]{2,1,0:T(8,128)(2,1)}, u32[]{:S(2)}) copy-start(bf16[1,160,1024]{2,1,0:T(8,128)(2,1)} %param.11) | copy-start | bytes 983044
  66.3 105.7 %all-to-all-start = ((bf16[8,160,128]{2,1,0:T(8,128)(2,1)}), bf16[8,160,128]{2,1,0:T(8,128)(2,1)S(1)}, u32[]{:S(2)}, u32[]{:S(2)}) async-start(bf16[8,160,128]{2,1,0:T(8,128)(2,1)} %bitcast.150), calls=%async_computation | async-start | bytes 655360 | tf_op jit(solution)/shard_map/all_to_all | solution.py:85
  119.7 56.4 %copy-start.2 = (s32[1,8]{1,0:T(1,128)S(1)}, s32[1,8]{1,0:T(1,128)}, u32[]{:S(2)}) copy-start(s32[1,8]{1,0:T(1,128)} %param.12) | copy-start | bytes 100
  119.7 57.0 %copy-start.1 = (bf16[1,31,1024]{2,1,0:T(8,128)(2,1)S(1)}, bf16[1,31,1024]{2,1,0:T(8,128)(2,1)}, u32[]{:S(2)}) copy-start(bf16[1,31,1024]{2,1,0:T(8,128)(2,1)} %param.18) | copy-start | bytes 190468
  172.0 28.9 %all-to-all-start.1 = ((bf16[8,160,256]{2,1,0:T(8,128)(2,1)}), bf16[8,160,256]{2,1,0:T(8,128)(2,1)S(1)}, u32[]{:S(2)}, u32[]{:S(2)}) async-start(bf16[8,160,256]{2,1,0:T(8,128)(2,1)} %maximum_bitcast_fusion), calls=%async_computation.1 | async-start | bytes 1310720 | tf_op jit(solution)/shard_map/all_to_all | solution.py:86
  175.5 186.5 %all-gather.23.cloned.1.call-start = ((), (), s32[]{:S(2)}) async-start(), calls=%async_computation.8 | async-start | bytes 2359296 | tf_op jit(solution)/shard_map/all_gather | solution.py:63
  238.6 19.5 %all-to-all-start.2 = ((bf16[8,160,128]{2,1,0:T(8,128)(2,1)}), bf16[8,160,128]{2,1,0:T(8,128)(2,1)S(1)}, u32[]{:S(2)}, u32[]{:S(2)}) async-start(bf16[8,160,128]{2,1,0:T(8,128)(2,1)} %reshape.468), calls=%async_computation.2 | async-start | bytes 655360 | tf_op jit(solution)/shard_map/all_to_all | solution.py:129
  314.0 5.0 %collective-permute-start = (bf16[15,1024]{1,0:T(8,128)(2,1)S(1)}, bf16[15,1024]{1,0:T(8,128)(2,1)S(1)}, u32[]{:S(2)}, u32[]{:S(2)}) collective-permute-start(bf16[15,1024]{1,0:T(8,128)(2,1)S(1)} %get-tuple-element.84), channel_id=1, source_target_pairs={{0,1},{1,2},{2,3},{3,4},{4,5},{5,6},{6,7},{8,9},{9,10},{10,11},{11... | collective-permute-start | bytes 92168 | tf_op jit(solution)/shard_map/ppermute | solution.py:17
  317.4 6.3 %collective-permute-start.1 = (bf16[15,1024]{1,0:T(8,128)(2,1)S(1)}, bf16[15,1024]{1,0:T(8,128)(2,1)S(1)}, u32[]{:S(2)}, u32[]{:S(2)}) collective-permute-start(bf16[15,1024]{1,0:T(8,128)(2,1)S(1)} %get-tuple-element.85), channel_id=1, source_target_pairs={{1,0},{2,1},{3,2},{4,3},{5,4},{6,5},{7,6},{9,8},{10,9},{11,10},{12... | collective-permute-start | bytes 92168 | tf_op jit(solution)/shard_map/ppermute | solution.py:20
  364.2 6.6 %collective-permute-start.2 = (bf16[160,1024]{1,0:T(8,128)(2,1)S(1)}, bf16[160,1024]{1,0:T(8,128)(2,1)S(1)}, u32[]{:S(2)}, u32[]{:S(2)}) collective-permute-start(bf16[160,1024]{1,0:T(8,128)(2,1)S(1)} %fusion.53), channel_id=1, source_target_pairs={{24,0},{0,8},{8,16},{16,24},{25,1},{1,9},{9,17},{17,25},{26,2},{2,... | collective-permute-start | bytes 983048 | tf_op jit(solution)/shard_map/ppermute | solution.py:28
Sparse Core Ops, SparseCore 0:
  9.4 53.7 all-gather.12
  65.2 52.1 all-gather.16
  119.5 49.2 all-gather.14
  170.7 57.7 all-gather.18
  230.4 80.2 all-gather.20
  312.6 49.3 all-gather.22
where the time goes:
time: 379 us; the launch traced here: 378 us
  waiting for transfers between devices  285 us (75%)
  matrix products  46 us (12%)
  starting transfers between devices  15.7 us (4%)
  between operations  13.8 us (4%)
  other arithmetic  10.2 us (3%)
  local copies, waits for them, and re-layouts  7.62 us (2%)
    all_gather x1, waiting for transfers between devices, body(): lax.all_gather(w_query[0], 'seq', axis=1, tiled=True)  50.9 us
    all_gather x1, waiting for transfers between devices, body(): lax.all_gather(conv_in[0], 'seq', axis=1, tiled=True)  50 us
    all_gather x1, waiting for transfers between devices, body(): lax.all_gather(w_key[0], 'seq', axis=1, tiled=True)  49.1 us
    all_gather x1, waiting for transfers between devices, body(): lax.all_gather(w_value[0], 'seq', axis=1, tiled=True)  47.7 us
    all_gather x1, waiting for transfers between devices, body(): lax.all_gather(conv_out[0], 'seq', axis=1, tiled=True)  34 us
    all_to_all x1, waiting for transfers between devices, body(): lax.all_to_all(copies, 'seq', split_axis=0, concat_axis=0, tiled=True)  22.7 us
    all_to_all x1, waiting for transfers between devices, body(): lax.all_to_all(outgoing, 'seq', split_axis=0, concat_axis=0, tiled=True)  15.6 us
    sub x5, matrix products, attend_block(): expw = jnp.where(allowed, jnp.exp(scores - peak), 0.0)  12.2 us
  transfers between devices with their start and end apart: 12, of which 9 were waited for; matrix products, arithmetic and copies ran while one was open for 16% of the time, Pallas kernels for 0%

commit v1 on v0

--- a/solution.py
+++ b/solution.py
@@ -35,7 +35,8 @@
 
 
 def segment_ids(positions, lengths):
-    bounds = jnp.cumsum(lengths)
+    order = jnp.arange(lengths.shape[0], dtype=jnp.int32)
+    bounds = jnp.sum(jnp.where(order[None, :] <= order[:, None], lengths[None, :], 0), axis=1)
     return jnp.sum((positions[:, None] >= bounds[None, :]).astype(jnp.int32), axis=1)
 
 

time: 379 us -> 379 us (level)
  no operation moved by 1% of the time
where the time goes in v1:
time: 379 us; the launch traced here: 378 us
  waiting for transfers between devices  285 us (75%)
  matrix products  46 us (12%)
  starting transfers between devices  15.7 us (4%)
  between operations  13.8 us (4%)
  other arithmetic  10.1 us (3%)
  local copies, waits for them, and re-layouts  7.62 us (2%)
    all_gather x1, waiting for transfers between devices, body(): lax.all_gather(w_query[0], 'seq', axis=1, tiled=True)  50.3 us
    all_gather x1, waiting for transfers between devices, body(): lax.all_gather(conv_in[0], 'seq', axis=1, tiled=True)  50 us
    all_gather x1, waiting for transfers between devices, body(): lax.all_gather(w_key[0], 'seq', axis=1, tiled=True)  49.1 us
    all_gather x1, waiting for transfers between devices, body(): lax.all_gather(w_value[0], 'seq', axis=1, tiled=True)  47.7 us
    all_gather x1, waiting for transfers between devices, body(): lax.all_gather(conv_out[0], 'seq', axis=1, tiled=True)  34 us
    all_to_all x1, waiting for transfers between devices, body(): lax.all_to_all(copies, 'seq', split_axis=0, concat_axis=0, tiled=True)  23.4 us
    all_to_all x1, waiting for transfers between devices, body(): lax.all_to_all(outgoing, 'seq', split_axis=0, concat_axis=0, tiled=True)  15.6 us
    sub x5, matrix products, attend_block(): expw = jnp.where(allowed, jnp.exp(scores - peak), 0.0)  12.2 us
  transfers between devices with their start and end apart: 12, of which 9 were waited for; matrix products, arithmetic and copies ran while one was open for 16% of the time, Pallas kernels for 0%

profile of v1, /device:TPU:0, one launch (start us, length us, event | category | flops | bytes accessed | tf_op | source)
XLA Modules:
  0.0 378.4 jit_solution(5965705355667393853)
XLA Ops:
  12.9 50.3 %all-gather.13.cloned.1.call-done = bf16[1,1024,1024]{2,1,0:T(8,128)(2,1)} async-done(((bf16[1,1024,128]{2,1,0:T(8,128)(2,1)}), bf16[1,1024,1024]{2,1,0:T(8,128)(2,1)}) %all-gather.13.cloned.1.call-update) | async-done | bytes 2097168 | tf_op jit(solution)/shard_map/all_gather | solution.py:59
  63.2 2.3 fusion.71
  66.3 3.4 all-to-all-start
  69.8 47.7 %all-gather.17.cloned.1.call-done = bf16[1,1024,1024]{2,1,0:T(8,128)(2,1)} async-done(((bf16[1,1024,128]{2,1,0:T(8,128)(2,1)}), bf16[1,1024,1024]{2,1,0:T(8,128)(2,1)}) %all-gather.17.cloned.1.call-update) | async-done | bytes 2097168 | tf_op jit(solution)/shard_map/all_gather | solution.py:61
  117.5 2.2 fusion.65
  119.7 49.1 %all-gather.15.cloned.1.call-done = bf16[1,1024,1024]{2,1,0:T(8,128)(2,1)} async-done(((bf16[1,1024,128]{2,1,0:T(8,128)(2,1)}), bf16[1,1024,1024]{2,1,0:T(8,128)(2,1)}) %all-gather.15.cloned.1.call-update) | async-done | bytes 2097168 | tf_op jit(solution)/shard_map/all_gather | solution.py:60
  168.8 2.1 fusion.68
  172.0 3.5 all-to-all-start.1
  177.5 23.4 %all-to-all-done.1 = bf16[8,160,256]{2,1,0:T(8,128)(2,1)S(1)} async-done(((bf16[8,160,256]{2,1,0:T(8,128)(2,1)}), bf16[8,160,256]{2,1,0:T(8,128)(2,1)S(1)}, u32[]{:S(2)}, u32[]{:S(2)}) %all-to-all-start.1) | async-done | bytes 655392 | tf_op jit(solution)/shard_map/all_to_all | solution.py:87
  202.8 33.4 %while.10 = (s32[]{:T(128)}, bf16[5,256,2,64]{1,3,2,0:T(8,128)(2,1)}, s32[5,256]{1,0:T(8,128)S(1)}, s32[1280]{0:T(1024)S(1)}, bf16[5,256,2,64]{1,3,2,0:T(8,128)(...) while((s32[]{:T(128)}, bf16[5,256,2,64]{1,3,2,0:T(8,128)(2,1)}, ...), condition=%wide.region_8.9_spmd, body=%wide.region_5.8_spmd.sunk | while | flops 258608128 | bytes 10696281 | solution.py:122
  203.0 1.7 fusion.160
  204.7 2.4 fusion.161
  207.2 2.3 fusion.162
  211.4 2.4 fusion.161
  213.8 2.3 fusion.162
  218.1 2.4 fusion.161
  220.5 2.3 fusion.162
  224.7 2.4 fusion.161
  227.2 2.3 fusion.162
  231.4 2.4 fusion.161
  233.8 2.3 fusion.162
  238.6 3.6 all-to-all-start.2
  242.4 15.6 %all-to-all-done.2 = bf16[8,160,128]{2,1,0:T(8,128)(2,1)S(1)} async-done(((bf16[8,160,128]{2,1,0:T(8,128)(2,1)}), bf16[8,160,128]{2,1,0:T(8,128)(2,1)S(1)}, u32[]{:S(2)}, u32[]{:S(2)}) %all-to-all-start.2) | async-done | bytes 327712 | tf_op jit(solution)/shard_map/all_to_all | solution.py:130
  258.2 2.2 fusion.138
  260.7 50.0 %all-gather.21.cloned.1.call-done = bf16[1,1024,2048]{2,1,0:T(8,128)(2,1)} async-done(((bf16[1,1024,256]{2,1,0:T(8,128)(2,1)}), bf16[1,1024,2048]{2,1,0:T(8,128)(2,1)}) %all-gather.21.cloned.1.call-update) | async-done | bytes 4194320 | tf_op jit(solution)/shard_map/all_gather | solution.py:63
  310.7 3.1 fusion.35
  314.0 3.4 collective-permute-start
  319.0 4.7 %collective-permute-done.1 = bf16[15,1024]{1,0:T(8,128)(2,1)S(1)} collective-permute-done((bf16[15,1024]{1,0:T(8,128)(2,1)S(1)}, bf16[15,1024]{1,0:T(8,128)(2,1)S(1)}, u32[]{:S(2)}, u32[]{:S(2)}) %collective-permute-start.1) | collective-permute-done | bytes 30752 | tf_op jit(solution)/shard_map/ppermute | solution.py:20
  323.7 4.1 %fusion.132 = (f32[160]{0:T(256)S(1)}, f32[160,1024]{1,0:T(8,128)S(1)}) fusion(f32[1024]{0:T(1024)S(1)} %bitcast.190, bf16[15,1024]{1,0:T(8,128)(2,1)S(1)} %collective-permute-done.1, bf16[160,1024]{1,0:T(8,128)(2,1)S(1)} %fusion.83, pred[160]{0:T(512)(128)(4,1)S(1)} %get-tuple-element.146, f32[1024]{0:T(1024)S(1)} %bitcast.191, ...), kind=kLoop, calls=%fused_computation.241 | loop fusion | flops 34897760 | bytes 1176896 | tf_op jit(solution)/shard_map/reduce_sum | solution.py:32
  328.0 34.0 %all-gather.23.cloned.1.call-done = bf16[1,1024,1024]{2,1,0:T(8,128)(2,1)} async-done(((bf16[1,1024,128]{2,1,0:T(8,128)(2,1)}), bf16[1,1024,1024]{2,1,0:T(8,128)(2,1)}) %all-gather.23.cloned.1.call-update) | async-done | bytes 2097168 | tf_op jit(solution)/shard_map/all_gather | solution.py:64
  362.0 2.2 fusion.53
  364.3 6.5 %collective-permute-done.2 = bf16[160,1024]{1,0:T(8,128)(2,1)S(1)} collective-permute-done((bf16[160,1024]{1,0:T(8,128)(2,1)S(1)}, bf16[160,1024]{1,0:T(8,128)(2,1)S(1)}, u32[]{:S(2)}, u32[]{:S(2)}) %collective-permute-start.2) | collective-permute-done | bytes 327712 | tf_op jit(solution)/shard_map/ppermute | solution.py:28
  (77 shorter events, 25.7 us)
Async XLA Ops:
  6.5 56.7 %all-gather.13.cloned.1.call-start = ((), (), s32[]{:S(2)}) async-start(), calls=%async_computation.3 | async-start | bytes 2359296 | tf_op jit(solution)/shard_map/all_gather | solution.py:59
  7.3 110.2 %all-gather.17.cloned.1.call-start = ((), (), s32[]{:S(2)}) async-start(), calls=%async_computation.5 | async-start | bytes 2359296 | tf_op jit(solution)/shard_map/all_gather | solution.py:61
  8.0 160.8 %all-gather.15.cloned.1.call-start = ((), (), s32[]{:S(2)}) async-start(), calls=%async_computation.4 | async-start | bytes 2359296 | tf_op jit(solution)/shard_map/all_gather | solution.py:60
  8.7 249.5 %all-gather.19.cloned.1.call-start = ((), (), s32[]{:S(2)}) async-start(), calls=%async_computation.6 | async-start | bytes 2359296 | tf_op jit(solution)/shard_map/all_gather | solution.py:62
  9.3 301.4 %all-gather.21.cloned.1.call-start = ((), (), s32[]{:S(2)}) async-start(), calls=%async_computation.7 | async-start | bytes 4718592 | tf_op jit(solution)/shard_map/all_gather | solution.py:63
  9.9 352.1 %all-gather.23.cloned.1.call-start = ((), (), s32[]{:S(2)}) async-start(), calls=%async_computation.8 | async-start | bytes 2359296 | tf_op jit(solution)/shard_map/all_gather | solution.py:64
  10.5 107.0 %copy-start = (bf16[1,160,1024]{2,1,0:T(8,128)(2,1)S(1)}, bf16[1,160,1024]{2,1,0:T(8,128)(2,1)}, u32[]{:S(2)}) copy-start(bf16[1,160,1024]{2,1,0:T(8,128)(2,1)} %param.11) | copy-start | bytes 983044
  66.3 105.7 %all-to-all-start = ((bf16[8,160,128]{2,1,0:T(8,128)(2,1)}), bf16[8,160,128]{2,1,0:T(8,128)(2,1)S(1)}, u32[]{:S(2)}, u32[]{:S(2)}) async-start(bf16[8,160,128]{2,1,0:T(8,128)(2,1)} %bitcast.149), calls=%async_computation | async-start | bytes 655360 | tf_op jit(solution)/shard_map/all_to_all | solution.py:86
  119.7 55.9 %copy-start.2 = (s32[1,8]{1,0:T(1,128)S(1)}, s32[1,8]{1,0:T(1,128)}, u32[]{:S(2)}) copy-start(s32[1,8]{1,0:T(1,128)} %param.12) | copy-start | bytes 100
  119.7 56.3 %copy-start.1 = (bf16[1,31,1024]{2,1,0:T(8,128)(2,1)S(1)}, bf16[1,31,1024]{2,1,0:T(8,128)(2,1)}, u32[]{:S(2)}) copy-start(bf16[1,31,1024]{2,1,0:T(8,128)(2,1)} %param.18) | copy-start | bytes 190468
  172.0 28.9 %all-to-all-start.1 = ((bf16[8,160,256]{2,1,0:T(8,128)(2,1)}), bf16[8,160,256]{2,1,0:T(8,128)(2,1)S(1)}, u32[]{:S(2)}, u32[]{:S(2)}) async-start(bf16[8,160,256]{2,1,0:T(8,128)(2,1)} %maximum_bitcast_fusion), calls=%async_computation.1 | async-start | bytes 1310720 | tf_op jit(solution)/shard_map/all_to_all | solution.py:87
  238.6 19.5 %all-to-all-start.2 = ((bf16[8,160,128]{2,1,0:T(8,128)(2,1)}), bf16[8,160,128]{2,1,0:T(8,128)(2,1)S(1)}, u32[]{:S(2)}, u32[]{:S(2)}) async-start(bf16[8,160,128]{2,1,0:T(8,128)(2,1)} %reshape.443), calls=%async_computation.2 | async-start | bytes 655360 | tf_op jit(solution)/shard_map/all_to_all | solution.py:130
  314.0 5.0 %collective-permute-start = (bf16[15,1024]{1,0:T(8,128)(2,1)S(1)}, bf16[15,1024]{1,0:T(8,128)(2,1)S(1)}, u32[]{:S(2)}, u32[]{:S(2)}) collective-permute-start(bf16[15,1024]{1,0:T(8,128)(2,1)S(1)} %get-tuple-element.84), channel_id=1, source_target_pairs={{0,1},{1,2},{2,3},{3,4},{4,5},{5,6},{6,7},{8,9},{9,10},{10,11},{11... | collective-permute-start | bytes 92168 | tf_op jit(solution)/shard_map/ppermute | solution.py:17
  317.4 6.3 %collective-permute-start.1 = (bf16[15,1024]{1,0:T(8,128)(2,1)S(1)}, bf16[15,1024]{1,0:T(8,128)(2,1)S(1)}, u32[]{:S(2)}, u32[]{:S(2)}) collective-permute-start(bf16[15,1024]{1,0:T(8,128)(2,1)S(1)} %get-tuple-element.85), channel_id=1, source_target_pairs={{1,0},{2,1},{3,2},{4,3},{5,4},{6,5},{7,6},{9,8},{10,9},{11,10},{12... | collective-permute-start | bytes 92168 | tf_op jit(solution)/shard_map/ppermute | solution.py:20
  364.2 6.6 %collective-permute-start.2 = (bf16[160,1024]{1,0:T(8,128)(2,1)S(1)}, bf16[160,1024]{1,0:T(8,128)(2,1)S(1)}, u32[]{:S(2)}, u32[]{:S(2)}) collective-permute-start(bf16[160,1024]{1,0:T(8,128)(2,1)S(1)} %fusion.53), channel_id=1, source_target_pairs={{24,0},{0,8},{8,16},{16,24},{25,1},{1,9},{9,17},{17,25},{26,2},{2,... | collective-permute-start | bytes 983048 | tf_op jit(solution)/shard_map/ppermute | solution.py:28
Sparse Core Ops, SparseCore 0:
  9.4 53.7 all-gather.12
  65.2 52.1 all-gather.16
  119.5 49.2 all-gather.14
  170.7 57.7 all-gather.18
  230.4 80.2 all-gather.20
  312.6 49.3 all-gather.22

commit v2 on v1

--- a/solution.py
+++ b/solution.py
@@ -1,12 +1,16 @@
+import functools
 import math
 
 import jax
 import jax.numpy as jnp
 from jax import lax
+from jax.experimental import pallas as pl
+from jax.experimental.pallas import tpu as pltpu
 from jax.sharding import PartitionSpec as P
 
 HEADS = 16
 KERNEL = 31
+MESH = pl.DeviceIdType.MESH
 
 
 def padded_2(block, sides, width):
@@ -40,9 +44,234 @@
     return jnp.sum((positions[:, None] >= bounds[None, :]).astype(jnp.int32), axis=1)
 
 
-def body(frames, lengths, w_query, w_key, w_value, w_output, conv_in, conv_taps, conv_out):
-    hidden = frames[0]
-    utt_lengths = lengths[0]
+def ring_index(place, shards):
+    place = lax.rem(place + shards, shards)
+    late = lax.div(place, shards // 2)
+    return (1 - late) * (2 * place) + late * (2 * (shards - 1 - place) + 1)
+
+
+def attention_kernel(
+    shards,
+    head_size,
+    frames_ref,
+    seg_row_ref,
+    seg_col_ref,
+    query_ref,
+    key_ref,
+    value_ref,
+    w_a_ref,
+    w_b_ref,
+    w_c_ref,
+    attended_ref,
+    full_a_ref,
+    full_b_ref,
+    full_c_ref,
+    normed,
+    query,
+    keys,
+    values,
+    outbox,
+    send_sem,
+    recv_sem,
+    own_sem,
+    out_send,
+    out_recv,
+):
+    rows = frames_ref.shape[0]
+    width = query_ref.shape[1]
+    steps = shards // 2
+    me = lax.axis_index("seq")
+    odd = lax.rem(me, 2)
+    place = (1 - odd) * lax.div(me, 2) + odd * (shards - 1 - lax.div(me, 2))
+    right, left = ring_index(place + 1, shards), ring_index(place - 1, shards)
+
+    barrier = pltpu.get_barrier_semaphore()
+    for away in range(1, shards):
+        peer = lax.rem(me + away, shards)
+        pl.semaphore_signal(barrier, inc=1, device_id={"seq": peer}, device_id_type=MESH)
+
+    own_rows = pl.ds(pl.multiple_of(me * rows, rows), rows)
+    normed[own_rows, :] = layer_norm(frames_ref[...].astype(jnp.float32)).astype(jnp.bfloat16)
+    pl.semaphore_wait(barrier, shards - 1)
+
+    pairs = ((w_a_ref, full_a_ref), (w_b_ref, full_b_ref), (w_c_ref, full_c_ref))
+
+    def view(load, owner, half):
+        if load == 0:
+            first, size = (0, rows) if half is None else (half * (rows // 2), rows // 2)
+            return normed.at[pl.ds(pl.multiple_of(owner * rows + first, 16), size), :]
+        own, full = pairs[load - 1]
+        depth, part = own.shape
+        first, size = (0, depth) if half is None else (half * (depth // 2), depth // 2)
+        return full.at[pl.ds(first, size), pl.ds(pl.multiple_of(owner * part, 128), part)]
+
+    def hop(load, step, way):
+        half = way if step == steps - 1 else None
+        owner = ring_index(place - step if way == 0 else place + step, shards)
+        target = view(load, owner, half)
+        source = target
+        if load > 0 and step == 0:
+            source = pairs[load - 1][0]
+            if half is not None:
+                depth = source.shape[0] // 2
+                source = source.at[pl.ds(half * depth, depth), :]
+        return pltpu.make_async_remote_copy(
+            src_ref=source,
+            dst_ref=target,
+            send_sem=send_sem.at[load, step, way],
+            recv_sem=recv_sem.at[load, step, way],
+            device_id={"seq": right if way == 0 else left},
+            device_id_type=MESH,
+        )
+
+    def arrive(load, step):
+        for way in range(2):
+            hop(load, step, way).wait_recv()
+
+    def send(load, step):
+        for way in range(2):
+            hop(load, step, way).start()
+
+    def project(owner):
+        at = pl.ds(pl.multiple_of(owner * rows, rows), rows)
+        block = normed[at, :]
+        query[at, :] = (
+            jnp.dot(block, query_ref[...], preferred_element_type=jnp.float32)
+            .astype(jnp.bfloat16)
+        ) * jnp.bfloat16(1.0 / math.sqrt(head_size))
+        keys[at, :] = jnp.dot(
+            block, key_ref[...], preferred_element_type=jnp.float32
+        ).astype(jnp.bfloat16)
+        values[at, :] = jnp.dot(
+            block, value_ref[...], preferred_element_type=jnp.float32
+        ).astype(jnp.bfloat16)
+
+    kept = []
+    send(0, 0)
+    for load in (1, 2, 3):
+        own, full = pairs[load - 1]
+        part = own.shape[1]
+        copy = pltpu.make_async_copy(
+            own, full.at[:, pl.ds(pl.multiple_of(me * part, 128), part)], own_sem.at[load - 1]
+        )
+        copy.start()
+        kept.append(copy)
+    project(me)
+    for step in range(steps):
+        arrive(0, step)
+        if step < steps - 1:
+            send(0, step + 1)
+        if step == steps - 2:
+            for load in (1, 2, 3):
+                send(load, 0)
+        project(ring_index(place - 1 - step, shards))
+        if step < steps - 1:
+            project(ring_index(place + 1 + step, shards))
+
+    lane = lax.broadcasted_iota(jnp.int32, (rows, width), 1)
+    my_columns = pl.ds(pl.multiple_of(me * width, 128), width)
+
+    def attend(owner):
+        at = pl.ds(pl.multiple_of(owner * rows, rows), rows)
+        block = query[at, :]
+        allowed = seg_row_ref[at, :] == seg_col_ref[...]
+        result = jnp.zeros((rows, width), jnp.float32)
+        for head in range(width // head_size):
+            mine = (lane >= head * head_size) & (lane < (head + 1) * head_size)
+            scores = lax.dot_general(
+                jnp.where(mine, block, jnp.bfloat16(0)),
+                keys[...],
+                (((1,), (1,)), ((), ())),
+                preferred_element_type=jnp.float32,
+            )
+            scores = jnp.where(allowed, scores, -1e30)
+            peak = jnp.max(scores, axis=1, keepdims=True)
+            expw = jnp.exp(scores - peak)
+            total = jnp.sum(expw, axis=1, keepdims=True)
+            mixed = jnp.dot(
+                expw.astype(jnp.bfloat16), values[...], preferred_element_type=jnp.float32
+            )
+            result = jnp.where(mine, mixed / total, result)
+        return result.astype(jnp.bfloat16)
+
+    def out_copy(away):
+        peer = lax.rem(me + away, shards)
+        return pltpu.make_async_remote_copy(
+            src_ref=outbox.at[away - 1],
+            dst_ref=attended_ref.at[:, my_columns],
+            send_sem=out_send.at[away - 1],
+            recv_sem=out_recv.at[away - 1],
+            device_id={"seq": peer},
+            device_id_type=MESH,
+        )
+
+    later = [(load, step) for step in range(steps) for load in (1, 2, 3)]
+    moved = 0
+
+    def forward(load, step):
+        arrive(load, step)
+        if step < steps - 1:
+            send(load, step + 1)
+
+    for away in range(1, shards + 1):
+        if away < shards:
+            outbox[away - 1] = attend(lax.rem(me + away, shards))
+            out_copy(away).start()
+        else:
+            attended_ref[:, my_columns] = attend(me)
+        if away * 4 % shards == 0 and away < shards:
+            forward(*later[moved])
+            moved += 1
+    for load, step in later[moved:]:
+        forward(load, step)
+    for away in range(1, shards):
+        out_copy(away).wait()
+    for copy in kept:
+        copy.wait()
+    for load in range(4):
+        for step in range(steps):
+            for way in range(2):
+                hop(load, step, way).wait_send()
+
+
+def attention_call(shards, hidden, segments, w_query, w_key, w_value, rest):
+    rows, depth = hidden.shape
+    width = w_query.shape[1]
+    total = rows * shards
+    steps = shards // 2
+    vmem = pl.BlockSpec(memory_space=pltpu.VMEM)
+    anywhere = pl.BlockSpec(memory_space=pl.ANY)
+    dma = pltpu.SemaphoreType.DMA
+    return pl.pallas_call(
+        functools.partial(attention_kernel, shards, depth // HEADS),
+        out_shape=[jax.ShapeDtypeStruct((rows, shards * width), jnp.bfloat16)]
+        + [jax.ShapeDtypeStruct((w.shape[0], w.shape[1] * shards), w.dtype) for w in rest],
+        in_specs=[vmem] * 6 + [anywhere] * 3,
+        out_specs=[vmem] + [anywhere] * 3,
+        scratch_shapes=[
+            pltpu.VMEM((total, depth), jnp.bfloat16),
+            pltpu.VMEM((total, width), jnp.bfloat16),
+            pltpu.VMEM((total, width), jnp.bfloat16),
+            pltpu.VMEM((total, width), jnp.bfloat16),
+            pltpu.VMEM((shards - 1, rows, width), jnp.bfloat16),
+            dma((4, steps, 2)),
+            dma((4, steps, 2)),
+            dma((3,)),
+            dma((shards - 1,)),
+            dma((shards - 1,)),
+        ],
+        compiler_params=pltpu.CompilerParams(
+            collective_id=0, has_side_effects=True, vmem_limit_bytes=48 * 1024 * 1024
+        ),
+        cost_estimate=pl.CostEstimate(
+            flops=2 * total * width * (3 * depth + 4 * total),
+            bytes_accessed=20_000_000,
+            transcendentals=total * total * 2,
+        ),
+    )(hidden, segments[:, None], segments[None, :], w_query, w_key, w_value, *rest)
+
+
+def attention_general(hidden, utt_lengths, w_query, w_key, w_value, w_output, conv_in, conv_out):
     shards = lax.axis_size("seq")
     my_index = lax.axis_index("seq")
     local_rows = hidden.shape[0]
@@ -56,12 +285,12 @@
     part_rows = local_rows // parts
     group_width = group_heads * head_size
     full_query, full_key, full_value, full_output, full_conv_in, full_conv_out = (
-        lax.all_gather(w_query[0], "seq", axis=1, tiled=True),
-        lax.all_gather(w_key[0], "seq", axis=1, tiled=True),
-        lax.all_gather(w_value[0], "seq", axis=1, tiled=True),
-        lax.all_gather(w_output[0], "seq", axis=1, tiled=True),
-        lax.all_gather(conv_in[0], "seq", axis=1, tiled=True),
-        lax.all_gather(conv_out[0], "seq", axis=1, tiled=True),
+        lax.all_gather(w_query, "seq", axis=1, tiled=True),
+        lax.all_gather(w_key, "seq", axis=1, tiled=True),
+        lax.all_gather(w_value, "seq", axis=1, tiled=True),
+        lax.all_gather(w_output, "seq", axis=1, tiled=True),
+        lax.all_gather(conv_in, "seq", axis=1, tiled=True),
+        lax.all_gather(conv_out, "seq", axis=1, tiled=True),
     )
     normed = layer_norm(hidden.astype(jnp.float32)).astype(jnp.bfloat16)
     query = jnp.dot(normed, full_query, preferred_element_type=jnp.float32).astype(jnp.bfloat16)
@@ -133,6 +362,39 @@
         .transpose(1, 2, 0, 3)
         .reshape(local_rows, width)
     )
+    return attended_local, full_output, full_conv_in, full_conv_out
+
+
+def body(frames, lengths, w_query, w_key, w_value, w_output, conv_in, conv_taps, conv_out):
+    hidden = frames[0]
+    utt_lengths = lengths[0]
+    shards = lax.axis_size("seq")
+    my_index = lax.axis_index("seq")
+    local_rows = hidden.shape[0]
+    width = hidden.shape[1]
+    total_rows = local_rows * shards
+    if shards % 2 == 0 and width // shards == 128 and local_rows % 32 == 0:
+        segments = segment_ids(jnp.arange(total_rows, dtype=jnp.int32), utt_lengths)
+        attended_local, full_output, full_conv_in, full_conv_out = attention_call(
+            shards,
+            hidden,
+            segments,
+            w_query[0],
+            w_key[0],
+            w_value[0],
+            (w_output[0], conv_in[0], conv_out[0]),
+        )
+    else:
+        attended_local, full_output, full_conv_in, full_conv_out = attention_general(
+            hidden,
+            utt_lengths,
+            w_query[0],
+            w_key[0],
+            w_value[0],
+            w_output[0],
+            conv_in[0],
+            conv_out[0],
+        )
     after_attn = hidden.astype(jnp.float32) + jnp.dot(
         attended_local, full_output, preferred_element_type=jnp.float32
     )

time: 379 us -> 153 us (0.40)
  waiting for transfers between devices: 285 us -> 11.6 us
  Pallas kernels: 0 us -> 118 us
  matrix products: 46 us -> 4.65 us
  between operations: 13.8 us -> 0.21 us
  starting transfers between devices: 15.7 us -> 4.58 us
  other arithmetic: 10.1 us -> 6.11 us
    all_gather x6 -> x0, waiting for transfers between devices: 231 us -> none  [the longest x1 50.3 us: body(): lax.all_gather(w_query[0], 'seq', axis=1, tiled=True)]
    pallas_call x0 -> x1, Pallas kernels: none -> 118 us  [attention_call(): pl.pallas_call(functools.partial(attention_kernel, shards, depth // HEADS...]
    all_to_all x3 -> x0, waiting for transfers between devices: 39 us -> none  [the longest x1 23.4 us: body(): lax.all_to_all(copies, 'seq', split_axis=0, concat_axis=0, tiled=True)]
    dot_general x13 -> x0, matrix products: 26.4 us -> none  [the longest x5 11.5 us: attend_block(): jnp.einsum('hqk,khd->hqd', expw.astype(jnp.bfloat16), value_rows, preferr...]
    sub x5 -> x0, matrix products: 12.2 us -> none  [attend_block(): expw = jnp.where(allowed, jnp.exp(scores - peak), 0.0)]
    all_to_all x3 -> x0, starting transfers between devices: 10.6 us -> none  [the longest x1 3.62 us: body(): lax.all_to_all(outgoing, 'seq', split_axis=0, concat_axis=0, tiled=True)]
    unnamed x8 -> x19, local copies, waits for them, and re-layouts: 0.8 us -> 7.49 us
  transfers between devices with their start and end apart: 12 -> 3, of which waited for: 9 -> 2; matrix products, arithmetic and copies ran while one was open for 16% -> 0% of each run, Pallas kernels for 0% -> 0%
where the time goes in v2:
time: 153 us
  Pallas kernels  118 us (77%)
  waiting for transfers between devices  11.6 us (8%)
  local copies, waits for them, and re-layouts  7.73 us (5%)
  other arithmetic  6.11 us (4%)
  matrix products  4.65 us (3%)
  starting transfers between devices  4.58 us (3%)
    pallas_call x1, Pallas kernels, attention_call(): pl.pallas_call(functools.partial(attention_kernel, shards, depth // HEADS...  118 us
    unnamed x19, local copies, waits for them, and re-layouts  7.49 us
    ppermute x1, waiting for transfers between devices, passed_along(): return lax.ppermute(block, axis, route)  6.49 us
    ppermute x1, waiting for transfers between devices, padded_2(): lax.ppermute(lax.slice_in_dim(block, 0, width, axis=dim), axis, backward)  5.13 us
    reduce_sum x1, other arithmetic, layer_norm(): centre = values - jnp.mean(values, axis=-1, keepdims=True)  4.1 us
    dot_general x1, matrix products, body(): jnp.dot(conv_normed, full_conv_in, preferred_element_type=jnp.float32)  3.33 us
    ppermute x1, starting transfers between devices, padded_2(): lax.ppermute(lax.slice_in_dim(block, block.shape[dim] - width, None, axis...  3.24 us
  transfers between devices with their start and end apart: 3, of which 2 were waited for; matrix products, arithmetic and copies ran while one was open for 0% of the time, Pallas kernels for 0%

profile of v2, /device:TPU:0, one launch (start us, length us, event | category | flops | bytes accessed | tf_op | source)
XLA Modules:
  0.0 152.5 jit_solution(2213662343119574573)
XLA Ops:
  0.0 0.8 select_reduce_fusion
  0.8 0.1 convert_reduce_fusion
  0.9 0.2 broadcast_in_dim.333.seg_row_ref
  1.1 0.0 copy-start
  1.1 1.0 copy-done
  2.1 1.0 copy-done.1
  3.1 0.9 copy-done.2
  4.1 0.9 copy-done.3
  5.0 0.9 copy-done.4
  6.0 0.9 copy-done.5
  6.9 0.9 copy-done.6
  7.9 117.6 %shard_map.91 = (bf16[160,1024]{1,0:T(8,128)(2,1)S(1)}, bf16[1024,1024]{1,0:T(8,128)(2,1)S(1)}, bf16[1024,2048]{1,0:T(8,128)(2,1)}, bf16[1024,1024]{1,0:T(8,128)(2,1)}) custom-call(bf16[160,1024]{1,0:T(8,128)(2,1)S(1)} %bitcast.45, s32[1280,1]{1,0:T(8,128)S(1)} %broadcast_in_dim.333.seg_row_ref, s32[1,1280]{1,0:T(1,128)S(1)} %broadcast_in_dim.299.seg_col_ref, ...), custom_call_target="tpu_custom_call" | custom-call | flops 2684354560 | bytes 20000000 | tf_op jit(solution)/shard_map/pallas_call | solution.py:245
  125.5 0.6 fusion.43
  126.2 0.2 multiply_reduce_fusion.1
  126.4 0.0 copy-start.7
  126.4 3.3 %fusion.6 = f32[160,2048]{1,0:T(8,128)S(1)} fusion(bf16[1024,2048]{1,0:T(8,128)(2,1)} %get-tuple-element.11, f32[160,1024]{1,0:T(8,128)S(1)} %get-tuple-element.79, f32[160]{0:T(256)S(1)} %add_rsqrt_fusion.1, f32[160]{0:T(256)S(1)} %broadcast_multiply_fusion.1), kind=kOutput, calls=%fused_computation.42 | convolution fusion | flops 671580160 | bytes 6161664 | tf_op jit(solution)/shard_map/dot_general | solution.py:402
  129.8 0.2 fusion.5
  130.0 3.2 %collective-permute-start = (bf16[15,1024]{1,0:T(8,128)(2,1)S(1)}, bf16[15,1024]{1,0:T(8,128)(2,1)S(1)}, u32[]{:S(2)}, u32[]{:S(2)}) collective-permute-start(bf16[15,1024]{1,0:T(8,128)(2,1)S(1)} %get-tuple-element.15), channel_id=1, source_target_pairs={{0,1},{1,2},{2,3},{3,4},{4,5},{5,6},{6,7},{8,9},{9,10},{10,11},{11... | collective-permute-start | bytes 92168 | tf_op jit(solution)/shard_map/ppermute | solution.py:21
  133.2 1.3 collective-permute-start.1
  134.5 0.1 convert_reduce_fusion.1
  134.6 0.1 slice_compare_fusion.29
  134.7 0.1 slice_compare_fusion.28
  134.8 0.1 slice_compare_fusion.27
  134.9 0.1 slice_convert_fusion.30
  135.0 0.1 slice_compare_fusion.26
  135.1 5.1 %collective-permute-done.1 = bf16[15,1024]{1,0:T(8,128)(2,1)S(1)} collective-permute-done((bf16[15,1024]{1,0:T(8,128)(2,1)S(1)}, bf16[15,1024]{1,0:T(8,128)(2,1)S(1)}, u32[]{:S(2)}, u32[]{:S(2)}) %collective-permute-start.1) | collective-permute-done | bytes 30752 | tf_op jit(solution)/shard_map/ppermute | solution.py:24
  140.2 4.1 %fusion.41 = (f32[160]{0:T(256)S(1)}, f32[160,1024]{1,0:T(8,128)S(1)}) fusion(f32[1024]{0:T(1024)S(1)} %bitcast.82, bf16[15,1024]{1,0:T(8,128)(2,1)S(1)} %collective-permute-done.1, bf16[160,1024]{1,0:T(8,128)(2,1)S(1)} %fusion.5, pred[160]{0:T(512)(128)(4,1)S(1)} %get-tuple-element.77, f32[1024]{0:T(1024)S(1)} %bitcast.83, ...), kind=kLoop, calls=%fused_computation.170 | loop fusion | flops 34897760 | bytes 1176896 | tf_op jit(solution)/shard_map/reduce_sum | solution.py:36
  144.3 0.2 multiply_reduce_fusion
  144.6 0.7 fusion
  145.3 0.1 collective-permute-start.2
  145.3 6.5 %collective-permute-done.2 = bf16[160,1024]{1,0:T(8,128)(2,1)S(1)} collective-permute-done((bf16[160,1024]{1,0:T(8,128)(2,1)S(1)}, bf16[160,1024]{1,0:T(8,128)(2,1)S(1)}, u32[]{:S(2)}, u32[]{:S(2)}) %collective-permute-start.2) | collective-permute-done | bytes 327712 | tf_op jit(solution)/shard_map/ppermute | solution.py:32
  151.8 0.7 copy.13
  (19 shorter events, 0.1 us)
Async XLA Ops:
  1.1 1.0 copy-start
  2.1 1.0 copy-start.1
  3.1 0.9 copy-start.2
  4.1 0.9 copy-start.3
  5.0 0.9 copy-start.4
  6.0 0.9 copy-start.5
  6.9 0.9 copy-start.6
  126.4 8.5 %copy-start.7 = (bf16[1,31,1024]{2,1,0:T(8,128)(2,1)S(1)}, bf16[1,31,1024]{2,1,0:T(8,128)(2,1)}, u32[]{:S(2)}) copy-start(bf16[1,31,1024]{2,1,0:T(8,128)(2,1)} %param.16) | copy-start | bytes 190468
  129.8 14.8 %copy-start.8 = (bf16[1024,1024]{1,0:T(8,128)(2,1)S(1)}, bf16[1024,1024]{1,0:T(8,128)(2,1)}, u32[]{:S(2)}) copy-start(bf16[1024,1024]{1,0:T(8,128)(2,1)} %get-tuple-element.12) | copy-start | bytes 6291460
  130.0 5.1 %collective-permute-start = (bf16[15,1024]{1,0:T(8,128)(2,1)S(1)}, bf16[15,1024]{1,0:T(8,128)(2,1)S(1)}, u32[]{:S(2)}, u32[]{:S(2)}) collective-permute-start(bf16[15,1024]{1,0:T(8,128)(2,1)S(1)} %get-tuple-element.15), channel_id=1, source_target_pairs={{0,1},{1,2},{2,3},{3,4},{4,5},{5,6},{6,7},{8,9},{9,10},{10,11},{11... | collective-permute-start | bytes 92168 | tf_op jit(solution)/shard_map/ppermute | solution.py:21
  133.2 7.0 %collective-permute-start.1 = (bf16[15,1024]{1,0:T(8,128)(2,1)S(1)}, bf16[15,1024]{1,0:T(8,128)(2,1)S(1)}, u32[]{:S(2)}, u32[]{:S(2)}) collective-permute-start(bf16[15,1024]{1,0:T(8,128)(2,1)S(1)} %get-tuple-element.16), channel_id=1, source_target_pairs={{1,0},{2,1},{3,2},{4,3},{5,4},{6,5},{7,6},{9,8},{10,9},{11,10},{12... | collective-permute-start | bytes 92168 | tf_op jit(solution)/shard_map/ppermute | solution.py:24
  145.3 6.6 %collective-permute-start.2 = (bf16[160,1024]{1,0:T(8,128)(2,1)S(1)}, bf16[160,1024]{1,0:T(8,128)(2,1)S(1)}, u32[]{:S(2)}, u32[]{:S(2)}) collective-permute-start(bf16[160,1024]{1,0:T(8,128)(2,1)S(1)} %fusion), channel_id=1, source_target_pairs={{24,0},{0,8},{8,16},{16,24},{25,1},{1,9},{9,17},{17,25},{26,2},{2,... | collective-permute-start | bytes 983048 | tf_op jit(solution)/shard_map/ppermute | solution.py:32

commit v3 on v2

--- a/solution.py
+++ b/solution.py
@@ -50,22 +50,33 @@
     return (1 - late) * (2 * place) + late * (2 * (shards - 1 - place) + 1)
 
 
-def attention_kernel(
+def block_kernel(
     shards,
     head_size,
     frames_ref,
     seg_row_ref,
     seg_col_ref,
+    near_ref,
+    taps_ref,
     query_ref,
     key_ref,
     value_ref,
     w_a_ref,
     w_b_ref,
     w_c_ref,
-    attended_ref,
+    handed_ref,
+    hidden,
+    qkv,
     full_a_ref,
     full_b_ref,
     full_c_ref,
+    attended_ref,
+    after,
+    gates,
+    edge,
+    padded,
+    depthwise,
+    leaving,
     normed,
     query,
     keys,
@@ -76,9 +87,22 @@
     own_sem,
     out_send,
     out_recv,
+    in_sem,
+    edge_send,
+    edge_recv,
+    leave_send,
+    leave_recv,
 ):
     rows = frames_ref.shape[0]
+    depth = frames_ref.shape[1]
     width = query_ref.shape[1]
+    loads_in = [pltpu.make_async_copy(frames_ref, hidden, in_sem.at[3])]
+    for i, ref in enumerate((query_ref, key_ref, value_ref)):
+        loads_in.append(
+            pltpu.make_async_copy(ref, qkv.at[:, pl.ds(i * width, width)], in_sem.at[i])
+        )
+    for copy in loads_in:
+        copy.start()
     steps = shards // 2
     me = lax.axis_index("seq")
     odd = lax.rem(me, 2)
@@ -89,10 +113,17 @@
     for away in range(1, shards):
         peer = lax.rem(me + away, shards)
         pl.semaphore_signal(barrier, inc=1, device_id={"seq": peer}, device_id_type=MESH)
-
+    phase = lax.axis_index("phase")
+    phases = lax.axis_size("phase")
+    phase_next = lax.rem(phase + 1, phases)
+    phase_back = lax.rem(phase + phases - 1, phases)
+    for peer in (phase_next, phase_back):
+        pl.semaphore_signal(barrier, inc=1, device_id={"phase": peer}, device_id_type=MESH)
+
+    loads_in[0].wait()
     own_rows = pl.ds(pl.multiple_of(me * rows, rows), rows)
-    normed[own_rows, :] = layer_norm(frames_ref[...].astype(jnp.float32)).astype(jnp.bfloat16)
-    pl.semaphore_wait(barrier, shards - 1)
+    normed[own_rows, :] = layer_norm(hidden[...].astype(jnp.float32)).astype(jnp.bfloat16)
+    pl.semaphore_wait(barrier, shards + 1)
 
     pairs = ((w_a_ref, full_a_ref), (w_b_ref, full_b_ref), (w_c_ref, full_c_ref))
 
@@ -135,16 +166,10 @@
     def project(owner):
         at = pl.ds(pl.multiple_of(owner * rows, rows), rows)
         block = normed[at, :]
-        query[at, :] = (
-            jnp.dot(block, query_ref[...], preferred_element_type=jnp.float32)
-            .astype(jnp.bfloat16)
-        ) * jnp.bfloat16(1.0 / math.sqrt(head_size))
-        keys[at, :] = jnp.dot(
-            block, key_ref[...], preferred_element_type=jnp.float32
-        ).astype(jnp.bfloat16)
-        values[at, :] = jnp.dot(
-            block, value_ref[...], preferred_element_type=jnp.float32
-        ).astype(jnp.bfloat16)
+        both = jnp.dot(block, qkv[...], preferred_element_type=jnp.float32).astype(jnp.bfloat16)
+        query[at, :] = both[:, :width] * jnp.bfloat16(1.0 / math.sqrt(head_size))
+        keys[at, :] = both[:, width : 2 * width]
+        values[at, :] = both[:, 2 * width :]
 
     kept = []
     send(0, 0)
@@ -156,14 +181,16 @@
         )
         copy.start()
         kept.append(copy)
+    for copy in loads_in[1:]:
+        copy.wait()
     project(me)
     for step in range(steps):
         arrive(0, step)
         if step < steps - 1:
             send(0, step + 1)
         if step == steps - 2:
-            for load in (1, 2, 3):
-                send(load, 0)
+            send(1, 0)
+            send(2, 0)
         project(ring_index(place - 1 - step, shards))
         if step < steps - 1:
             project(ring_index(place + 1 + step, shards))
@@ -205,70 +232,186 @@
             device_id_type=MESH,
         )
 
-    later = [(load, step) for step in range(steps) for load in (1, 2, 3)]
-    moved = 0
-
     def forward(load, step):
         arrive(load, step)
         if step < steps - 1:
             send(load, step + 1)
 
+    first = [(load, step) for step in range(steps) for load in (1, 2)]
+    moved = 0
     for away in range(1, shards + 1):
         if away < shards:
             outbox[away - 1] = attend(lax.rem(me + away, shards))
             out_copy(away).start()
         else:
             attended_ref[:, my_columns] = attend(me)
-        if away * 4 % shards == 0 and away < shards:
-            forward(*later[moved])
+        if away * 4 % shards == 0 and away < shards and moved < 3:
+            forward(*first[moved])
             moved += 1
-    for load, step in later[moved:]:
+    send_last = False
+    for load, step in first[moved:-1]:
+        if load == 2 and step >= steps - 2:
+            continue
         forward(load, step)
+        if step >= steps - 2 and not send_last:
+            send(3, 0)
+            send_last = True
     for away in range(1, shards):
-        out_copy(away).wait()
+        out_copy(away).wait_recv()
     for copy in kept:
         copy.wait()
+    tile = 2 * width
+    for at in range(0, depth, tile):
+        cols = slice(at, at + tile)
+        after[:, cols] = hidden[:, cols].astype(jnp.float32) + jnp.dot(
+            attended_ref[...], full_a_ref[:, cols], preferred_element_type=jnp.float32
+        )
+    conv_normed = layer_norm(after[...]).astype(jnp.bfloat16)
+    part = w_b_ref.shape[1]
+
+    def gate(owner):
+        at = pl.ds(pl.multiple_of(owner * part, 128), part)
+        gates[:, at] = jnp.dot(
+            conv_normed, full_b_ref[:, at], preferred_element_type=jnp.float32
+        )
+
+    def gate_step(step):
+        gate(ring_index(place - 1 - step, shards))
+        if step < steps - 1:
+            gate(ring_index(place + 1 + step, shards))
+
+    gate(me)
+    for step in range(steps - 2):
+        gate_step(step)
+    forward(2, steps - 2)
+    gate_step(steps - 2)
+    forward(3, 0)
+    forward(2, steps - 1)
+    gate_step(steps - 1)
+    glu = (gates[:, :depth] * jax.nn.sigmoid(gates[:, depth:])).astype(jnp.bfloat16)
+    margin = edge.shape[1]
+    edge[0] = glu[:margin]
+    edge[1] = glu[rows - margin :]
+
+    def edge_copy(side):
+        peer = lax.rem(me + (shards - 1 if side == 0 else 1), shards)
+        return pltpu.make_async_remote_copy(
+            src_ref=edge.at[side],
+            dst_ref=edge.at[2 + side],
+            send_sem=edge_send.at[side],
+            recv_sem=edge_recv.at[side],
+            device_id={"seq": peer},
+            device_id_type=MESH,
+        )
+
+    edge_copy(0).start()
+    edge_copy(1).start()
+    padded[margin : margin + rows, :] = glu.astype(jnp.float32)
+    edge_copy(0).wait_recv()
+    edge_copy(1).wait_recv()
+    padded[:margin, :] = edge[3].astype(jnp.float32)
+    padded[margin + rows :, :] = edge[2].astype(jnp.float32)
+    moved_last = 1
+    reach = KERNEL // 2
+
+    def taps_of(at):
+        own = near_ref[margin : margin + rows, :]
+        summed = jnp.zeros((rows, 128), jnp.float32)
+        for offset in range(KERNEL):
+            start = margin - reach + offset
+            term = padded[start : start + rows, at : at + 128] * taps_ref[offset : offset + 1, at : at + 128]
+            keep = near_ref[start : start + rows, :] == own
+            summed = summed + jnp.where(keep, term, 0.0)
+        depthwise[:, at : at + 128] = summed
+
+    for at in range(0, depth, 128):
+        taps_of(at)
+        if at + 128 == depth // 2 and moved_last < steps - 1:
+            forward(3, moved_last)
+            moved_last += 1
+    conv_act = layer_norm(depthwise[...])
+    conv_act = (conv_act * jax.nn.sigmoid(conv_act)).astype(jnp.bfloat16)
+    for step in range(moved_last, steps):
+        forward(3, step)
+
+    def leave(piece):
+        cols = pl.ds(piece * tile, tile)
+        return pltpu.make_async_remote_copy(
+            src_ref=leaving.at[:, cols],
+            dst_ref=handed_ref.at[:, cols],
+            send_sem=leave_send.at[piece],
+            recv_sem=leave_recv.at[piece],
+            device_id={"phase": phase_next},
+            device_id_type=MESH,
+        )
+
+    for piece in range(depth // tile):
+        cols = slice(piece * tile, (piece + 1) * tile)
+        leaving[:, cols] = (
+            after[:, cols]
+            + jnp.dot(conv_act, full_c_ref[:, cols], preferred_element_type=jnp.float32)
+        ).astype(jnp.bfloat16)
+        leave(piece).start()
+    for away in range(1, shards):
+        out_copy(away).wait_send()
+    edge_copy(0).wait_send()
+    edge_copy(1).wait_send()
     for load in range(4):
         for step in range(steps):
             for way in range(2):
                 hop(load, step, way).wait_send()
-
-
-def attention_call(shards, hidden, segments, w_query, w_key, w_value, rest):
+    for piece in range(depth // tile):
+        leave(piece).wait()
+
+
+def block_call(shards, hidden, segments, near, taps, weights):
     rows, depth = hidden.shape
-    width = w_query.shape[1]
+    width = weights[0].shape[1]
     total = rows * shards
     steps = shards // 2
+    margin = (near.shape[0] - rows) // 2
     vmem = pl.BlockSpec(memory_space=pltpu.VMEM)
     anywhere = pl.BlockSpec(memory_space=pl.ANY)
     dma = pltpu.SemaphoreType.DMA
+    bf16, f32 = jnp.bfloat16, jnp.float32
     return pl.pallas_call(
-        functools.partial(attention_kernel, shards, depth // HEADS),
-        out_shape=[jax.ShapeDtypeStruct((rows, shards * width), jnp.bfloat16)]
-        + [jax.ShapeDtypeStruct((w.shape[0], w.shape[1] * shards), w.dtype) for w in rest],
-        in_specs=[vmem] * 6 + [anywhere] * 3,
-        out_specs=[vmem] + [anywhere] * 3,
+        functools.partial(block_kernel, shards, depth // HEADS),
+        out_shape=jax.ShapeDtypeStruct((rows, depth), bf16),
+        in_specs=[anywhere] + [vmem] * 4 + [anywhere] * 6,
+        out_specs=vmem,
         scratch_shapes=[
-            pltpu.VMEM((total, depth), jnp.bfloat16),
-            pltpu.VMEM((total, width), jnp.bfloat16),
-            pltpu.VMEM((total, width), jnp.bfloat16),
-            pltpu.VMEM((total, width), jnp.bfloat16),
-            pltpu.VMEM((shards - 1, rows, width), jnp.bfloat16),
+            pltpu.VMEM((rows, depth), bf16),
+            pltpu.VMEM((depth, 3 * width), bf16),
+        ]
+        + [pltpu.VMEM((w.shape[0], w.shape[1] * shards), bf16) for w in weights[3:]]
+        + [
+            pltpu.VMEM((rows, depth), bf16),
+            pltpu.VMEM((rows, depth), f32),
+            pltpu.VMEM((rows, 2 * depth), f32),
+            pltpu.VMEM((4, margin, depth), bf16),
+            pltpu.VMEM((rows + 2 * margin, depth), f32),
+            pltpu.VMEM((rows, depth), f32),
+            pltpu.VMEM((rows, depth), bf16),
+            pltpu.VMEM((total, depth), bf16),
+            pltpu.VMEM((total, width), bf16),
+            pltpu.VMEM((total, width), bf16),
+            pltpu.VMEM((total, width), bf16),
+            pltpu.VMEM((shards - 1, rows, width), bf16),
             dma((4, steps, 2)),
             dma((4, steps, 2)),
             dma((3,)),
             dma((shards - 1,)),
             dma((shards - 1,)),
+            dma((4,)),
+            dma((2,)),
+            dma((2,)),
+            dma((depth // (2 * width),)),
+            dma((depth // (2 * width),)),
         ],
         compiler_params=pltpu.CompilerParams(
-            collective_id=0, has_side_effects=True, vmem_limit_bytes=48 * 1024 * 1024
+            collective_id=0, has_side_effects=True, vmem_limit_bytes=56 * 1024 * 1024
         ),
-        cost_estimate=pl.CostEstimate(
-            flops=2 * total * width * (3 * depth + 4 * total),
-            bytes_accessed=20_000_000,
-            transcendentals=total * total * 2,
-        ),
-    )(hidden, segments[:, None], segments[None, :], w_query, w_key, w_value, *rest)
+    )(hidden, segments[:, None], segments[None, :], near, taps, *weights)
 
 
 def attention_general(hidden, utt_lengths, w_query, w_key, w_value, w_output, conv_in, conv_out):
@@ -373,28 +516,26 @@
     local_rows = hidden.shape[0]
     width = hidden.shape[1]
     total_rows = local_rows * shards
-    if shards % 2 == 0 and width // shards == 128 and local_rows % 32 == 0:
+    phases = lax.axis_size("phase")
+    if phases > 2 and shards % 8 == 0 and width // shards == 128 and local_rows % 32 == 0:
         segments = segment_ids(jnp.arange(total_rows, dtype=jnp.int32), utt_lengths)
-        attended_local, full_output, full_conv_in, full_conv_out = attention_call(
+        margin = 16
+        near_pos = my_index * local_rows - margin
+        near_pos = near_pos + jnp.arange(local_rows + 2 * margin, dtype=jnp.int32)
+        inside = (near_pos >= 0) & (near_pos < total_rows)
+        near = jnp.where(inside, segment_ids(near_pos, utt_lengths), -1)
+        handed = block_call(
             shards,
             hidden,
             segments,
-            w_query[0],
-            w_key[0],
-            w_value[0],
-            (w_output[0], conv_in[0], conv_out[0]),
-        )
-    else:
-        attended_local, full_output, full_conv_in, full_conv_out = attention_general(
-            hidden,
-            utt_lengths,
-            w_query[0],
-            w_key[0],
-            w_value[0],
-            w_output[0],
-            conv_in[0],
-            conv_out[0],
-        )
+            jnp.broadcast_to(near[:, None], (near.shape[0], 128)),
+            conv_taps[0].astype(jnp.float32),
+            (w_query[0], w_key[0], w_value[0], w_output[0], conv_in[0], conv_out[0]),
+        )
+        return handed[None]
+    attended_local, full_output, full_conv_in, full_conv_out = attention_general(
+        hidden, utt_lengths, w_query[0], w_key[0], w_value[0], w_output[0], conv_in[0], conv_out[0]
+    )
     after_attn = hidden.astype(jnp.float32) + jnp.dot(
         attended_local, full_output, preferred_element_type=jnp.float32
     )

time: 153 us -> 138 us (0.902)
  Pallas kernels: 118 us -> 132 us
  waiting for transfers between devices: 11.6 us -> 0 us
  other arithmetic: 6.11 us -> 0.97 us
  matrix products: 4.65 us -> 0 us
  starting transfers between devices: 4.58 us -> 0 us
  local copies, waits for them, and re-layouts: 7.73 us -> 4.76 us
    pallas_call x1, Pallas kernels: 118 us -> 132 us  [block_call(): pl.pallas_call(functools.partial(block_kernel, shards, depth // HEADS), o...]
    ppermute x3 -> x0, waiting for transfers between devices: 11.6 us -> none  [the longest x1 6.49 us: passed_along(): return lax.ppermute(block, axis, route)]
    unnamed x19 -> x5, local copies, waits for them, and re-layouts: 7.49 us -> 2.38 us
    dot_general x3 -> x0, matrix products: 4.65 us -> none  [the longest x1 3.33 us: body(): jnp.dot(conv_normed, full_conv_in, preferred_element_type=jnp.float32)]
    ppermute x3 -> x0, starting transfers between devices: 4.58 us -> none  [the longest x1 3.24 us: padded_2(): lax.ppermute(lax.slice_in_dim(block, block.shape[dim] - width, None, axis...]
    reduce_sum x3 -> x0, other arithmetic: 4.54 us -> none  [the longest x1 4.1 us: layer_norm(): centre = values - jnp.mean(values, axis=-1, keepdims=True)]
    broadcast_in_dim x2 -> x3, local copies, waits for them, and re-layouts: 0.23 us -> 2.39 us  [the longest x1 1.07 us: block_call(): segments[:, None]]
  transfers between devices with their start and end apart: 3 -> 0, of which waited for: 2 -> 0; matrix products, arithmetic and copies ran while one was open for 0% -> 0% of each run, Pallas kernels for 0% -> 0%
where the time goes in v3:
time: 138 us; the launch traced here: 137 us
  Pallas kernels  132 us (96%)
  local copies, waits for them, and re-layouts  4.76 us (3%)
    pallas_call x1, Pallas kernels, block_call(): pl.pallas_call(functools.partial(block_kernel, shards, depth // HEADS), o...  132 us

profile of v3, /device:TPU:0, one launch (start us, length us, event | category | flops | bytes accessed | tf_op | source)
XLA Modules:
  0.0 137.3 jit_solution(13512659688349138502)
XLA Ops:
  0.0 0.0 copy-start.1
  0.0 0.7 copy-done.1
  0.7 0.0 copy-start
  0.7 0.1 select_reduce_fusion
  0.8 0.1 convert_reduce_fusion.1
  0.9 0.1 convert_reduce_fusion
  1.0 0.6 broadcast_in_dim.49.seg_col_ref
  1.6 0.7 broadcast_in_dim.51.near_ref
  2.3 0.0 copy-done
  2.3 0.7 bitcast_convert_fusion.taps_ref
  3.0 1.1 broadcast_in_dim.53.seg_row_ref
  4.0 131.6 %shard_map.91 = bf16[160,1024]{1,0:T(8,128)(2,1)} custom-call(bf16[160,1024]{1,0:T(8,128)(2,1)} %bitcast.14, s32[1280,1]{1,0:T(8,128)} %broadcast_in_dim.53.seg_row_ref, s32[1,1280]{1,0:T(1,128)} %broadcast_in_dim.49.seg_col_ref, s32[192,128]{1,0:T(8,128)} %broadcast_in_dim.51.near_ref, f32[31,1024]{1,0:T(8,128)} %bitcast_convert_fusion.taps_ref, ...), custom_call_target="tpu_custom_call" | custom-call | tf_op jit(solution)/shard_map/pallas_call | solution.py:377
  135.6 1.7 %copy.13 = bf16[1,160,1024]{2,1,0:T(8,128)(2,1)} copy(bf16[1,160,1024]{2,1,0:T(8,128)(2,1)} %bitcast.12) | data formatting | bytes 655360
  (2 shorter events, 0.0 us)
Async XLA Ops:
  0.0 0.7 copy-start.1
  0.7 1.6 %copy-start = (bf16[1,31,1024]{2,1,0:T(8,128)(2,1)S(1)}, bf16[1,31,1024]{2,1,0:T(8,128)(2,1)}, u32[]{:S(2)}) copy-start(bf16[1,31,1024]{2,1,0:T(8,128)(2,1)} %param.16) | copy-start | bytes 190468

commit v4 on v3

--- a/solution.py
+++ b/solution.py
@@ -132,9 +132,9 @@
             first, size = (0, rows) if half is None else (half * (rows // 2), rows // 2)
             return normed.at[pl.ds(pl.multiple_of(owner * rows + first, 16), size), :]
         own, full = pairs[load - 1]
-        depth, part = own.shape
+        depth = own.shape[0]
         first, size = (0, depth) if half is None else (half * (depth // 2), depth // 2)
-        return full.at[pl.ds(first, size), pl.ds(pl.multiple_of(owner * part, 128), part)]
+        return full.at[owner, pl.ds(first, size), :]
 
     def hop(load, step, way):
         half = way if step == steps - 1 else None
@@ -175,10 +175,7 @@
     send(0, 0)
     for load in (1, 2, 3):
         own, full = pairs[load - 1]
-        part = own.shape[1]
-        copy = pltpu.make_async_copy(
-            own, full.at[:, pl.ds(pl.multiple_of(me * part, 128), part)], own_sem.at[load - 1]
-        )
+        copy = pltpu.make_async_copy(own, full.at[me], own_sem.at[load - 1])
         copy.start()
         kept.append(copy)
     for copy in loads_in[1:]:
@@ -261,10 +258,14 @@
     for copy in kept:
         copy.wait()
     tile = 2 * width
+
+    def joined(full, pair):
+        return jnp.concatenate([full[2 * pair], full[2 * pair + 1]], axis=1)
+
     for at in range(0, depth, tile):
         cols = slice(at, at + tile)
         after[:, cols] = hidden[:, cols].astype(jnp.float32) + jnp.dot(
-            attended_ref[...], full_a_ref[:, cols], preferred_element_type=jnp.float32
+            attended_ref[...], joined(full_a_ref, at // tile), preferred_element_type=jnp.float32
         )
     conv_normed = layer_norm(after[...]).astype(jnp.bfloat16)
     part = w_b_ref.shape[1]
@@ -272,7 +273,7 @@
     def gate(owner):
         at = pl.ds(pl.multiple_of(owner * part, 128), part)
         gates[:, at] = jnp.dot(
-            conv_normed, full_b_ref[:, at], preferred_element_type=jnp.float32
+            conv_normed, full_b_ref[owner], preferred_element_type=jnp.float32
         )
 
     def gate_step(step):
@@ -331,11 +332,9 @@
             moved_last += 1
     conv_act = layer_norm(depthwise[...])
     conv_act = (conv_act * jax.nn.sigmoid(conv_act)).astype(jnp.bfloat16)
-    for step in range(moved_last, steps):
-        forward(3, step)
-
-    def leave(piece):
-        cols = pl.ds(piece * tile, tile)
+
+    def leave(piece, owner):
+        cols = pl.ds(pl.multiple_of(owner * width, 128), width)
         return pltpu.make_async_remote_copy(
             src_ref=leaving.at[:, cols],
             dst_ref=handed_ref.at[:, cols],
@@ -345,13 +344,25 @@
             device_id_type=MESH,
         )
 
-    for piece in range(depth // tile):
-        cols = slice(piece * tile, (piece + 1) * tile)
+    sent = []
+
+    def finish(owner):
+        cols = pl.ds(pl.multiple_of(owner * width, 128), width)
         leaving[:, cols] = (
             after[:, cols]
-            + jnp.dot(conv_act, full_c_ref[:, cols], preferred_element_type=jnp.float32)
+            + jnp.dot(conv_act, full_c_ref[owner], preferred_element_type=jnp.float32)
         ).astype(jnp.bfloat16)
-        leave(piece).start()
+        copy = leave(len(sent), owner)
+        copy.start()
+        sent.append(copy)
+
+    finish(me)
+    for step in range(steps):
+        if step >= moved_last:
+            forward(3, step)
+        finish(ring_index(place - 1 - step, shards))
+        if step < steps - 1:
+            finish(ring_index(place + 1 + step, shards))
     for away in range(1, shards):
         out_copy(away).wait_send()
     edge_copy(0).wait_send()
@@ -360,8 +371,8 @@
         for step in range(steps):
             for way in range(2):
                 hop(load, step, way).wait_send()
-    for piece in range(depth // tile):
-        leave(piece).wait()
+    for copy in sent:
+        copy.wait()
 
 
 def block_call(shards, hidden, segments, near, taps, weights):
@@ -383,7 +394,7 @@
             pltpu.VMEM((rows, depth), bf16),
             pltpu.VMEM((depth, 3 * width), bf16),
         ]
-        + [pltpu.VMEM((w.shape[0], w.shape[1] * shards), bf16) for w in weights[3:]]
+        + [pltpu.VMEM((shards, *w.shape), bf16) for w in weights[3:]]
         + [
             pltpu.VMEM((rows, depth), bf16),
             pltpu.VMEM((rows, depth), f32),
@@ -405,8 +416,8 @@
             dma((4,)),
             dma((2,)),
             dma((2,)),
-            dma((depth // (2 * width),)),
-            dma((depth // (2 * width),)),
+            dma((shards,)),
+            dma((shards,)),
         ],
         compiler_params=pltpu.CompilerParams(
             collective_id=0, has_side_effects=True, vmem_limit_bytes=56 * 1024 * 1024

time: 138 us -> 137 us (level)
  no operation moved by 1% of the time
where the time goes in v4:
time: 137 us
  Pallas kernels  131 us (96%)
  local copies, waits for them, and re-layouts  4.76 us (3%)
    pallas_call x1, Pallas kernels, block_call(): pl.pallas_call(functools.partial(block_kernel, shards, depth // HEADS), o...  131 us

profile of v4, /device:TPU:0, one launch (start us, length us, event | category | flops | bytes accessed | tf_op | source)
XLA Modules:
  0.0 136.7 jit_solution(745308908185984217)
XLA Ops:
  0.0 0.0 copy-start.1
  0.0 0.7 copy-done.1
  0.7 0.0 copy-start
  0.7 0.1 select_reduce_fusion
  0.8 0.1 convert_reduce_fusion.1
  0.9 0.1 convert_reduce_fusion
  1.0 0.6 broadcast_in_dim.49.seg_col_ref
  1.6 0.7 broadcast_in_dim.51.near_ref
  2.3 0.0 copy-done
  2.3 0.7 bitcast_convert_fusion.taps_ref
  3.0 1.1 broadcast_in_dim.53.seg_row_ref
  4.0 130.9 %shard_map.91 = bf16[160,1024]{1,0:T(8,128)(2,1)} custom-call(bf16[160,1024]{1,0:T(8,128)(2,1)} %bitcast.14, s32[1280,1]{1,0:T(8,128)} %broadcast_in_dim.53.seg_row_ref, s32[1,1280]{1,0:T(1,128)} %broadcast_in_dim.49.seg_col_ref, s32[192,128]{1,0:T(8,128)} %broadcast_in_dim.51.near_ref, f32[31,1024]{1,0:T(8,128)} %bitcast_convert_fusion.taps_ref, ...), custom_call_target="tpu_custom_call" | custom-call | tf_op jit(solution)/shard_map/pallas_call | solution.py:388
  135.0 1.7 %copy.13 = bf16[1,160,1024]{2,1,0:T(8,128)(2,1)} copy(bf16[1,160,1024]{2,1,0:T(8,128)(2,1)} %bitcast.12) | data formatting | bytes 655360
  (2 shorter events, 0.0 us)
Async XLA Ops:
  0.0 0.7 copy-start.1
  0.7 1.6 %copy-start = (bf16[1,31,1024]{2,1,0:T(8,128)(2,1)S(1)}, bf16[1,31,1024]{2,1,0:T(8,128)(2,1)}, u32[]{:S(2)}) copy-start(bf16[1,31,1024]{2,1,0:T(8,128)(2,1)} %param.16) | copy-start | bytes 190468
